TPU v7x, 512 devices: a whole 4x8x8 slice. The times are simulated.
512 devices in a mesh: rows: 64 (over z, x, core), cols: 8 (over y).
Axes of the slice: x: 4, y: 8, z: 8, core: 2. Of those that a mesh axis runs over, the one named last changes fastest.
Arguments:
- cost: bfloat16 [28672, 28672], P('rows', 'cols'), may hold values from 0 to 1
- row_mass: float32 [28672], P('rows'), may hold values from 0.2 to 6
- col_mass: float32 [28672], P('cols'), may hold values from 0.2 to 6
- slab: bfloat16 [28672, 512], P('cols'), may hold values from -128 to 128
Outputs:
- aligned: bfloat16 [28672, 512], P('rows', 'cols')
All inputs are finite; a program needn't handle non-finite values.
Results may differ from a plain program's by a relative error of at most 0.0058.
Values sent between devices are 32-bit elements; how exact they have to be, the bound alone decides.
A program may use at most 64 MiB of HBM per device.

v0:
```python
import jax
import jax.numpy as jnp
from jax import lax
from jax.sharding import PartitionSpec as P

ITERS = 4


sharpness = 80.0


def make_kernel(cost):
    return jnp.exp(-sharpness * cost.astype(jnp.float32)).astype(jnp.bfloat16)


def on_device(cost, row_mass, col_mass, slab):
    stored_kernel = make_kernel(cost)

    def fetch_kernel():
        return stored_kernel

    col_scale = jnp.ones((cost.shape[1],), jnp.float32)
    row_scale = jnp.ones((cost.shape[0],), jnp.float32)
    for repeat in range(ITERS):
        partial_rows = jnp.dot(
            fetch_kernel(),
            col_scale,
            precision=lax.Precision.HIGHEST,
            preferred_element_type=jnp.float32,
        )
        row_sums = lax.psum(partial_rows, "cols")
        row_scale = row_mass / row_sums
        col_part = jnp.dot(
            row_scale,
            fetch_kernel(),
            precision=lax.Precision.HIGHEST,
            preferred_element_type=jnp.float32,
        )
        col_sums = lax.psum(col_part, "rows")
        col_scale = col_mass / col_sums
    scaled = (col_scale[:, None] * slab.astype(jnp.float32)).astype(jnp.bfloat16)
    term_block = jnp.dot(fetch_kernel(), scaled, preferred_element_type=jnp.float32)
    summed = lax.psum_scatter(term_block, "cols", scatter_dimension=1, tiled=True)
    return ((row_scale / row_mass)[:, None] * summed).astype(jnp.bfloat16)


def solution(mesh):
    return jax.shard_map(
        on_device,
        mesh=mesh,
        in_specs=(P("rows", "cols"), P("rows"), P("cols"), P("cols", None)),
        out_specs=P("rows", "cols"),
        check_vma=False,
    )
```

profile of v0, /device:TPU:6, one launch (start us, length us, event | category | flops | bytes accessed | tf_op | source)
XLA Modules:
  0.0 1130.5 jit_solution(16356028853292997763)
XLA Ops:
  6.5 0.0 copy-start.2
  6.5 0.0 copy-start.1
  6.5 0.0 copy-start
  6.5 0.0 reduce-scatter.2.cloned.1.call-start
  6.5 4.7 fusion.2
  11.3 17.6 %psum.56 = f32[448]{0:T(512)S(1)} all-reduce(f32[448]{0:T(512)S(1)} %bitcast.21), channel_id=1, replica_groups=mesh['rows'=64,'cols'=8] {'cols'}, use_global_device_ids=true, to_apply=%region_0.0 | all-reduce | flops 448 | bytes 3584 | tf_op jit(solution)/shard_map/psum | solution.py:31
  28.9 0.0 copy-done.1
  28.9 0.0 copy-done.2
  28.9 1.9 convolution_reduce_fusion.3
  30.8 238.2 %psum.57 = f32[3584]{0:T(1024)S(1)} all-reduce(f32[3584]{0:T(1024)S(1)} %convolution_reduce_fusion.3), channel_id=1, replica_groups=mesh['rows'=64,'cols'=8] {'rows'}, use_global_device_ids=true, to_apply=%region_1.0 | all-reduce | flops 3584 | bytes 28672 | tf_op jit(solution)/shard_map/psum | solution.py:39
  269.0 0.0 copy-done
  269.0 2.7 fusion.7
  271.7 15.0 %psum.58 = f32[448]{0:T(512)S(1)} all-reduce(f32[448]{0:T(512)S(1)} %bitcast.18), channel_id=1, replica_groups=mesh['rows'=64,'cols'=8] {'cols'}, use_global_device_ids=true, to_apply=%region_2.0 | all-reduce | flops 448 | bytes 3584 | tf_op jit(solution)/shard_map/psum | solution.py:31
  286.7 1.9 convolution_reduce_fusion.2
  288.6 246.1 %psum.59 = f32[3584]{0:T(1024)S(1)} all-reduce(f32[3584]{0:T(1024)S(1)} %convolution_reduce_fusion.2), channel_id=1, replica_groups=mesh['rows'=64,'cols'=8] {'rows'}, use_global_device_ids=true, to_apply=%region_3.0 | all-reduce | flops 3584 | bytes 28672 | tf_op jit(solution)/shard_map/psum | solution.py:39
  534.8 2.7 fusion.6
  537.5 15.5 %psum.60 = f32[448]{0:T(512)S(1)} all-reduce(f32[448]{0:T(512)S(1)} %bitcast.19), channel_id=1, replica_groups=mesh['rows'=64,'cols'=8] {'cols'}, use_global_device_ids=true, to_apply=%region_4.0 | all-reduce | flops 448 | bytes 3584 | tf_op jit(solution)/shard_map/psum | solution.py:31
  553.0 1.9 convolution_reduce_fusion.1
  554.9 246.1 %psum.61 = f32[3584]{0:T(1024)S(1)} all-reduce(f32[3584]{0:T(1024)S(1)} %convolution_reduce_fusion.1), channel_id=1, replica_groups=mesh['rows'=64,'cols'=8] {'rows'}, use_global_device_ids=true, to_apply=%region_5.0 | all-reduce | flops 3584 | bytes 28672 | tf_op jit(solution)/shard_map/psum | solution.py:39
  801.1 2.7 fusion.5
  803.8 15.0 %psum.62 = f32[448]{0:T(512)S(1)} all-reduce(f32[448]{0:T(512)S(1)} %bitcast.20), channel_id=1, replica_groups=mesh['rows'=64,'cols'=8] {'cols'}, use_global_device_ids=true, to_apply=%region_6.0 | all-reduce | flops 448 | bytes 3584 | tf_op jit(solution)/shard_map/psum | solution.py:31
  818.8 1.9 convolution_reduce_fusion
  820.7 246.1 %psum.63 = f32[3584]{0:T(1024)S(1)} all-reduce(f32[3584]{0:T(1024)S(1)} %convolution_reduce_fusion), channel_id=1, replica_groups=mesh['rows'=64,'cols'=8] {'rows'}, use_global_device_ids=true, to_apply=%region_7.0 | all-reduce | flops 3584 | bytes 28672 | tf_op jit(solution)/shard_map/psum | solution.py:39
  1066.8 6.2 fusion
  1073.0 0.0 reduce-scatter.2.cloned.1.call-update
  1073.1 49.0 %reduce-scatter.2.cloned.1.call-done = f32[448,64]{0,1:T(8,128)} async-done(((f32[448,512]{0,1:T(8,128)}), f32[448,64]{0,1:T(8,128)}) %reduce-scatter.2.cloned.1.call-update) | async-done | bytes 114704 | tf_op jit(solution)/shard_map/reduce_scatter | solution.py:43
  1122.1 1.5 multiply_convert_fusion.2
  (11 shorter events, 0.1 us)
Async XLA Ops:
  6.5 22.4 %copy-start.2 = (bf16[448,3584]{1,0:T(8,128)(2,1)S(1)}, bf16[448,3584]{1,0:T(8,128)(2,1)}, u32[]{:S(2)}) copy-start(bf16[448,3584]{1,0:T(8,128)(2,1)} %param.4) | copy-start | bytes 9633796
  6.5 22.4 %copy-start.1 = (f32[448]{0:T(512)S(1)}, f32[448]{0:T(512)}, u32[]{:S(2)}) copy-start(f32[448]{0:T(512)} %param.5) | copy-start | bytes 5380
  6.5 262.5 %copy-start = (f32[3584]{0:T(1024)S(1)}, f32[3584]{0:T(1024)}, u32[]{:S(2)}) copy-start(f32[3584]{0:T(1024)} %param.6) | copy-start | bytes 43012
  6.5 1115.6 %reduce-scatter.2.cloned.1.call-start = ((), (), s32[]{:S(2)}) async-start(), calls=%async_computation.1 | async-start | bytes 1179648 | tf_op jit(solution)/shard_map/reduce_scatter | solution.py:43
Sparse Core Ops, SparseCore 0:
  1073.2 48.8 reduce-scatter.1
where the time goes:
time: 1130 us
  blocking collectives  1040 us (92%)
  waiting for transfers between devices  49.1 us (4%)
  matrix products  26.6 us (2%)
  between operations  13.5 us (1%)
    psum x4, blocking collectives, on_device(): col_sums = lax.psum(col_part, 'rows')  977 us
    psum x4, blocking collectives, on_device(): row_sums = lax.psum(partial_rows, 'cols')  63.1 us
    reduce_scatter x1, waiting for transfers between devices, on_device(): lax.psum_scatter(term_block, 'cols', scatter_dimension=1, tiled=True)  49 us
  transfers between devices with their start and end apart: 1, of which 1 were waited for; matrix products, arithmetic and copies ran while one was open for 0% of the time, Pallas kernels for 0%

commit v1 on v0

v1 whole, which is shorter than its diff:
```python
import functools

import jax
import jax.numpy as jnp
from jax import lax
from jax.experimental import pallas as pl
from jax.experimental.pallas import tpu as pltpu
from jax.sharding import PartitionSpec as P

ITERS = 4
SHARPNESS = 80.0
MESH = pl.DeviceIdType.MESH
F32, BF16 = jnp.float32, jnp.bfloat16
NT = (((1,), (1,)), ((), ()))
TN = (((0,), (0,)), ((), ()))

ROWS, COLS, SLAB = 448, 3584, 512
NY = 8
OWN = SLAB // NY
CHUNKS = 2
CW = COLS // CHUNKS
TILES = CW // 128
TR = 16
LOADS = 7
LR = ROWS // LOADS
KC = 896
HALF = ROWS // 4
ORDER = (4, 3, 5, 2, 6, 1, 7)


def parent(s):
    return s + 1 if s < 0 else s - 1


def tree(h):
    left, right = (4, 3) if h == 0 else (3, 4)
    return [-s for s in range(left, 0, -1)] + list(range(right, 0, -1))


def split2(x):
    hi = x.astype(BF16).astype(F32)
    return hi, x - hi


def kernel(cost_ref, rm_ref, cm_ref, slab_ref, out_ref,
           k_ref, kr_ref, slab_v, acc_ref, t_ref, rbuf, racc, rb_ref, c2, left,
           ysrc, ydst, xsrc, xdst, zsrc, zdst,
           cost_sem, slab_sem, ysend, yrecv, xsend, xrecv, zsend, zrecv, fsend, frecv):
    r = lax.axis_index("rows")
    y = lax.axis_index("cols")
    lo = lax.rem(r, 8)

    def ypeer(d):
        return (r, lax.rem(y + d, 8))

    def xpeer(d):
        return (r - lo + lax.rem(lo + d, 8), y)

    def zpeer(d):
        return (lax.rem(r + 8 * d, 64), y)

    barrier = pltpu.get_barrier_semaphore()
    for peer in (ypeer, xpeer, zpeer):
        for d in ORDER:
            pl.semaphore_signal(barrier, inc=1, device_id=peer(d), device_id_type=MESH)

    def load(i):
        s = pl.ds(i * LR, LR)
        return pltpu.make_async_copy(cost_ref.at[s], k_ref.at[s], cost_sem.at[i])

    for i in range(LOADS):
        load(i).start()
    slab_copy = pltpu.make_async_copy(slab_ref, slab_v, slab_sem)
    slab_copy.start()

    left[...] = jnp.zeros_like(left)
    xsrc[...] = jnp.ones_like(xsrc)
    ysrc[...] = jnp.zeros_like(ysrc)

    for i in range(LOADS):
        load(i).wait()

        def exp_rows(j, carry, i=i):
            s = pl.ds(pl.multiple_of(i * LR + j * 32, 32), 32)
            k = jnp.exp(-SHARPNESS * k_ref[s, :].astype(F32)).astype(BF16)
            k_ref[s, :] = k
            k = k.astype(F32)
            total = k[:, 0:128]
            for q in range(1, COLS // 128):
                total = total + k[:, 128 * q:128 * (q + 1)]
            racc[s, :] = total
            return carry

        lax.fori_loop(0, LR // 32, exp_rows, 0)

    first = lax.dot_general(jnp.ones((8, 128), F32), racc[...], NT,
                            precision=lax.Precision.HIGHEST, preferred_element_type=F32)
    ysrc[0, :, 0:ROWS] = first[0:1]
    pl.semaphore_wait(barrier, 21)

    row8 = lax.broadcasted_iota(jnp.int32, (8, 1), 0)

    def two_rows(x):
        hi, rest = split2(x)
        return jnp.where(row8 == 0, hi, jnp.where(row8 == 1, rest, 0.0)).astype(BF16)

    def iteration(t, carry):
        for d in ORDER:
            pltpu.make_async_remote_copy(ysrc.at[t], ydst.at[t, d - 1], ysend.at[t], yrecv.at[t],
                                         device_id=ypeer(d), device_id_type=MESH).start()
        pltpu.make_async_copy(ydst.at[t], ydst.at[t], yrecv.at[t]).wait()
        sums = ysrc[t, :, 0:ROWS]
        for d in range(7):
            sums = sums + ydst[t, d, :, 0:ROWS]
        r2 = two_rows(rm_ref[...] / sums)

        for c in range(CHUNKS):
            part = jnp.dot(r2, k_ref[:, c * CW:(c + 1) * CW], preferred_element_type=F32)
            part = part[0:1] + part[1:2]
            for j in range(TILES):
                xsrc[t, c, j:j + 1, :] = part[:, 128 * j:128 * (j + 1)]
            for d in ORDER:
                pltpu.make_async_remote_copy(xsrc.at[t, c], xdst.at[t, c, d - 1], xsend.at[t], xrecv.at[t, c],
                                             device_id=xpeer(d), device_id_type=MESH).start()

        @pl.when(t == ITERS - 1)
        def _():
            r_over = two_rows(1.0 / sums)
            rb_ref[...] = lax.dot_general(r_over, jnp.ones((8, 128), BF16), TN, preferred_element_type=F32)

            def scale_rows(i, carry):
                s = pl.ds(pl.multiple_of(i * 32, 32), 32)
                rb = rb_ref[s, :]
                for q in range(COLS // 128):
                    kr_ref[s, 128 * q:128 * (q + 1)] = k_ref[s, 128 * q:128 * (q + 1)].astype(F32) * rb
                return carry

            lax.fori_loop(0, ROWS // 32, scale_rows, 0)

        for c in range(CHUNKS):
            pltpu.make_async_copy(xdst.at[t, c], xdst.at[t, c], xrecv.at[t, c]).wait()
            total = xsrc[t, c]
            for d in range(7):
                total = total + xdst[t, c, d]
            zsrc[t, c] = total
            for d in ORDER:
                pltpu.make_async_remote_copy(zsrc.at[t, c], zdst.at[t, c, d - 1], zsend.at[t], zrecv.at[t, c],
                                             device_id=zpeer(d), device_id_type=MESH).start()
        for c in range(CHUNKS):
            pltpu.make_async_copy(zdst.at[t, c], zdst.at[t, c], zrecv.at[t, c]).wait()
            total = zsrc[t, c]
            for d in range(7):
                total = total + zdst[t, c, d]
            scale = cm_ref[c] / total
            hi, rest = split2(scale)
            c2[0] = hi
            c2[1] = rest
            for j in range(TILES):
                lanes = pl.ds(c * CW + 128 * j, 128)
                left[0:1, lanes] = c2[0, j:j + 1, :]
                left[1:2, lanes] = c2[1, j:j + 1, :]

        @pl.when(t < ITERS - 1)
        def _():
            sums = jnp.zeros((8, ROWS), F32)
            for c in range(CHUNKS):
                s = slice(c * CW, (c + 1) * CW)
                sums = sums + lax.dot_general(left[:, s].astype(BF16), k_ref[:, s], NT, preferred_element_type=F32)
            ysrc[t + 1, :, 0:ROWS] = sums[0:1] + sums[1:2]

        return carry

    lax.fori_loop(0, ITERS, iteration, 0)

    slab_copy.wait()
    acc_ref[...] = jnp.zeros_like(acc_ref)

    def product(i, carry):
        s = pl.ds(pl.multiple_of(i * KC, KC), KC)
        scale = left[0:1, s] + left[1:2, s]
        plan = (kr_ref[:, s] * scale).astype(BF16)
        acc_ref[...] += jnp.dot(plan, slab_v[s, :], preferred_element_type=F32)
        return carry

    lax.fori_loop(0, COLS // KC, product, 0)

    def pack(i, carry):
        rows = pl.ds(pl.multiple_of(i * 32, 32), 32)
        below = pl.ds(pl.multiple_of(i * 32 + ROWS // 2, 32), 32)
        for p in range(NY // 2):
            lanes = slice(128 * p, 128 * (p + 1))
            top, bottom = acc_ref[rows, lanes], acc_ref[below, lanes]
            t_ref[2 * p, rows, :] = jnp.concatenate([top[:, :OWN], bottom[:, :OWN]], axis=1)
            t_ref[2 * p + 1, rows, :] = jnp.concatenate([top[:, OWN:], bottom[:, OWN:]], axis=1)
        return carry

    lax.fori_loop(0, ROWS // 64, pack, 0)

    nodes = [(h, s) for m in (4, 3, 2, 1) for h in (0, 1) for s in tree(h) if abs(s) == m]

    def slot(h, s):
        return tree(h).index(s)

    def hop(h, s):
        rows = pl.ds(h * HALF, HALF)
        dest = lax.rem(y - s + 8, 8)
        return pltpu.make_async_remote_copy(
            t_ref.at[dest, rows], rbuf.at[h, slot(h, s)], fsend.at[h, slot(h, s)], frecv.at[h, slot(h, s)],
            device_id=ypeer((parent(s) - s) % 8), device_id_type=MESH)

    def arrived(h, s):
        pltpu.make_async_copy(rbuf.at[h, slot(h, s)], rbuf.at[h, slot(h, s)], frecv.at[h, slot(h, s)]).wait()

    for h, s in nodes:
        rows = slice(h * HALF, (h + 1) * HALF)
        dest = lax.rem(y - s + 8, 8)
        for child in tree(h):
            if parent(child) == s:
                arrived(h, child)
                t_ref[dest, rows, :] = t_ref[dest, rows, :] + rbuf[h, slot(h, child)]
        hop(h, s).start()
    for h in (0, 1):
        rows = slice(h * HALF, (h + 1) * HALF)
        total = t_ref[y, rows, :]
        for child in tree(h):
            if parent(child) == 0:
                arrived(h, child)
                total = total + rbuf[h, slot(h, child)]
        total = total.astype(BF16)
        out_ref[h * HALF:(h + 1) * HALF, :] = total[:, :OWN]
        out_ref[ROWS // 2 + h * HALF:ROWS // 2 + (h + 1) * HALF, :] = total[:, OWN:]

    for t in range(ITERS):
        pltpu.make_async_copy(ydst.at[t], ydst.at[t], ysend.at[t]).wait()
        pltpu.make_async_copy(xdst.at[t], xdst.at[t], xsend.at[t]).wait()
        pltpu.make_async_copy(zdst.at[t], zdst.at[t], zsend.at[t]).wait()
    for h, s in nodes:
        hop(h, s).wait_send()


def on_device(cost, row_mass, col_mass, slab):
    masses = col_mass.reshape(CHUNKS, TILES, 128)
    masses = jnp.pad(masses, ((0, 0), (0, TR - TILES), (0, 0)), constant_values=1.0)
    vmem = pl.BlockSpec(memory_space=pltpu.VMEM)
    hbm = pl.BlockSpec(memory_space=pl.ANY)
    dma = pltpu.SemaphoreType.DMA
    return pl.pallas_call(
        kernel,
        out_shape=jax.ShapeDtypeStruct((ROWS, OWN), BF16),
        in_specs=[hbm, vmem, vmem, hbm],
        out_specs=vmem,
        scratch_shapes=[
            pltpu.VMEM((ROWS, COLS), BF16),
            pltpu.VMEM((ROWS, COLS), F32),
            pltpu.VMEM((COLS, SLAB), BF16),
            pltpu.VMEM((ROWS, SLAB), F32),
            pltpu.VMEM((NY, ROWS // 2, 128), F32),
            pltpu.VMEM((2, 7, HALF, 128), F32),
            pltpu.VMEM((ROWS, 128), F32),
            pltpu.VMEM((ROWS, 128), F32),
            pltpu.VMEM((2, TR, 128), F32),
            pltpu.VMEM((8, COLS), F32),
            pltpu.VMEM((ITERS, 1, 512), F32),
            pltpu.VMEM((ITERS, 7, 1, 512), F32),
            pltpu.VMEM((ITERS, CHUNKS, TR, 128), F32),
            pltpu.VMEM((ITERS, CHUNKS, 7, TR, 128), F32),
            pltpu.VMEM((ITERS, CHUNKS, TR, 128), F32),
            pltpu.VMEM((ITERS, CHUNKS, 7, TR, 128), F32),
            dma((LOADS,)), dma,
            dma((ITERS,)), dma((ITERS,)),
            dma((ITERS,)), dma((ITERS, CHUNKS)),
            dma((ITERS,)), dma((ITERS, CHUNKS)),
            dma((2, 7)), dma((2, 7)),
        ],
        compiler_params=pltpu.CompilerParams(
            collective_id=0, has_side_effects=True, vmem_limit_bytes=48 * 2**20),
    )(cost, row_mass.reshape(1, ROWS), masses, slab)


def solution(mesh):
    return jax.shard_map(
        on_device,
        mesh=mesh,
        in_specs=(P("rows", "cols"), P("rows"), P("cols"), P("cols", None)),
        out_specs=P("rows", "cols"),
        check_vma=False,
    )
```

time: 1130 us -> 98.6 us (0.09)
  blocking collectives: 1040 us -> 0 us
  Pallas kernels: 0 us -> 94.2 us
  waiting for transfers between devices: 49.1 us -> 0 us
  matrix products: 26.6 us -> 0 us
  between operations: 13.5 us -> 0.01 us
    psum x8 -> x0, blocking collectives: 1040 us -> none  [the longest x4 977 us: on_device(): col_sums = lax.psum(col_part, 'rows')]
    pallas_call x0 -> x1, Pallas kernels: none -> 94.2 us  [on_device(): pl.pallas_call(kernel, out_shape=jax.ShapeDtypeStruct((ROWS, OWN), BF16),...]
    reduce_scatter x1 -> x0, waiting for transfers between devices: 49 us -> none  [on_device(): lax.psum_scatter(term_block, 'cols', scatter_dimension=1, tiled=True)]
    dot_general x9 -> x0, matrix products: 26.6 us -> none  [the longest x4 12.8 us: on_device(): jnp.dot(fetch_kernel(), col_scale, precision=lax.Precision.HIGHEST, prefe...]
  transfers between devices with their start and end apart: 1 -> 0, of which waited for: 1 -> 0; matrix products, arithmetic and copies ran while one was open for 0% -> 0% of each run, Pallas kernels for 0% -> 0%
where the time goes in v1:
time: 98.6 us; the launch traced here: 98.3 us
  Pallas kernels  94.2 us (96%)
  local copies, waits for them, and re-layouts  4.04 us (4%)
    pallas_call x1, Pallas kernels, on_device(): pl.pallas_call(kernel, out_shape=jax.ShapeDtypeStruct((ROWS, OWN), BF16),...  94.2 us
    unnamed x4, local copies, waits for them, and re-layouts  2.59 us

profile of v1, /device:TPU:6, one launch (start us, length us, event | category | flops | bytes accessed | tf_op | source)
XLA Modules:
  0.0 98.3 jit_solution(17543754061102511900)
XLA Ops:
  0.0 0.7 reshape.7
  0.7 0.0 copy-start
  0.7 1.9 %copy-done = bf16[448,3584]{1,0:T(8,128)(2,1)S(1)} copy-done((bf16[448,3584]{1,0:T(8,128)(2,1)S(1)}, bf16[448,3584]{1,0:T(8,128)(2,1)}, u32[]{:S(2)}) %copy-start) | copy-done | bytes 3211288
  2.6 0.0 copy-start.1
  2.6 0.7 copy-done.1
  3.3 94.2 %shard_map.46 = bf16[448,64]{1,0:T(8,128)(2,1)S(1)} custom-call(bf16[448,3584]{1,0:T(8,128)(2,1)S(1)} %copy-done, f32[1,448]{1,0:T(1,128)S(1)} %bitcast.1, f32[2,16,128]{2,1,0:T(8,128)S(1)} %pad.4.cm_ref, bf16[3584,512]{1,0:T(8,128)(2,1)} %slab_ref.1), custom_call_target="tpu_custom_call" | custom-call | tf_op jit(solution)/shard_map/pallas_call | solution.py:247
  97.6 0.7 copy.6
  (1 shorter events, 0.0 us)
Async XLA Ops:
  0.7 1.9 %copy-start = (bf16[448,3584]{1,0:T(8,128)(2,1)S(1)}, bf16[448,3584]{1,0:T(8,128)(2,1)}, u32[]{:S(2)}) copy-start(bf16[448,3584]{1,0:T(8,128)(2,1)} %cost_ref.1) | copy-start | bytes 9633796
  2.6 0.7 copy-start.1

commit v2 on v1

v2 whole, which is shorter than its diff:
```python
import functools

import jax
import jax.numpy as jnp
from jax import lax
from jax.experimental import pallas as pl
from jax.experimental.pallas import tpu as pltpu
from jax.sharding import PartitionSpec as P

ITERS = 4
SHARPNESS = 80.0
MESH = pl.DeviceIdType.MESH
F32, BF16 = jnp.float32, jnp.bfloat16
NT = (((1,), (1,)), ((), ()))
TN = (((0,), (0,)), ((), ()))

ROWS, COLS, SLAB = 448, 3584, 512
NY = 8
OWN = SLAB // NY
CW = COLS // 2
TILES = CW // 128
TR = 16
LOADS = 7
LR = ROWS // LOADS
KC = 896
PR = ROWS // 8
ORDER = (4, 3, 5, 2, 6, 1, 7)
GROUP = tuple((other, dx, dz) for other in (0, 1) for dx, dz in
              ((2, 1), (2, 0), (1, 1), (3, 1), (1, 0), (3, 0), (0, 1), (0, 0)) if (other, dx, dz) != (0, 0, 0))


def parent(s):
    if abs(s) == 4:
        return s // 2
    return s + 1 if s < 0 else s - 1


def tree(p):
    left, right = (4, 3) if p % 2 == 0 else (3, 4)
    return [-s for s in range(left, 0, -1)] + list(range(right, 0, -1))


def split2(x):
    hi = x.astype(BF16).astype(F32)
    return hi, x - hi


def kernel(cost_ref, rm_hbm, cm_hbm, slab_ref, out_ref,
           k_ref, kr_ref, slab_v, acc_ref, t_ref, rbuf, racc, rb_ref, c2, left, rm_ref, cm_row, cm_ref,
           ysrc, ydst, xsrc, xdst, zsrc, zdst,
           cost_sem, slab_sem, mass_sem, ysend, yrecv, xsend, xrecv, zsend, zrecv, fsend, frecv):
    r = lax.axis_index("rows")
    y = lax.axis_index("cols")
    z = r // 8
    x = lax.rem(r, 8) // 2
    core = lax.rem(r, 2)
    odd = lax.rem(z, 2)
    sign = 2 * odd - 1

    def ypeer(d):
        return (r, lax.rem(y + d, 8))

    def place(to_z, to_x, to_core):
        return (to_z * 8 + to_x * 2 + to_core, y)

    def gpeer(other, dx, dz):
        to_core = core + other * (1 - 2 * core)
        return place(z - dz * sign, lax.rem(x + dx, 4), to_core)

    def zpeer(other, k):
        to_core = core + other * (1 - 2 * core)
        return place(lax.rem(z + k * sign + 8, 8), x, to_core)

    barrier = pltpu.get_barrier_semaphore()

    def greet(peer):
        pl.semaphore_signal(barrier, inc=1, device_id=peer, device_id_type=MESH)

    for d in ORDER:
        greet(ypeer(d))
    for other, dx, dz in GROUP:
        greet(gpeer(other, dx, dz))
    for k in (1, 2, 3, -2):
        for other in (0, 1):
            greet(zpeer(other, k))

    def load(i):
        s = pl.ds(i * LR, LR)
        return pltpu.make_async_copy(cost_ref.at[s], k_ref.at[s], cost_sem.at[i])

    for i in range(LOADS):
        load(i).start()
    rm_copy = pltpu.make_async_copy(rm_hbm, rm_ref, mass_sem.at[0])
    cm_copy = pltpu.make_async_copy(cm_hbm, cm_row, mass_sem.at[1])
    slab_copy = pltpu.make_async_copy(slab_ref, slab_v, slab_sem)
    rm_copy.start()
    cm_copy.start()
    slab_copy.start()

    left[...] = jnp.zeros_like(left)
    xsrc[...] = jnp.ones_like(xsrc)
    ysrc[...] = jnp.zeros_like(ysrc)
    cm_ref[...] = jnp.ones_like(cm_ref)

    for i in range(LOADS):
        load(i).wait()

        def exp_rows(j, carry, i=i):
            s = pl.ds(pl.multiple_of(i * LR + j * 32, 32), 32)
            k = jnp.exp(-SHARPNESS * k_ref[s, :].astype(F32)).astype(BF16)
            k_ref[s, :] = k
            k = k.astype(F32)
            total = k[:, 0:128]
            for q in range(1, COLS // 128):
                total = total + k[:, 128 * q:128 * (q + 1)]
            racc[s, :] = total
            return carry

        lax.fori_loop(0, LR // 32, exp_rows, 0)

    first = lax.dot_general(jnp.ones((8, 128), F32), racc[...], NT,
                            precision=lax.Precision.HIGHEST, preferred_element_type=F32)
    ysrc[0, :, 0:ROWS] = first[0:1]
    pl.semaphore_wait(barrier, 7 + len(GROUP) + 8)
    rm_copy.wait()
    cm_copy.wait()

    row8 = lax.broadcasted_iota(jnp.int32, (8, 1), 0)

    def two_rows(v):
        hi, rest = split2(v)
        return jnp.where(row8 == 0, hi, jnp.where(row8 == 1, rest, 0.0)).astype(BF16)

    def iteration(t, carry):
        for d in ORDER:
            pltpu.make_async_remote_copy(ysrc.at[t], ydst.at[t, d - 1], ysend.at[t], yrecv.at[t],
                                         device_id=ypeer(d), device_id_type=MESH).start()

        @pl.when(t == 0)
        def _():
            for h in range(2):
                for j in range(TILES):
                    cm_ref[h, j:j + 1, :] = cm_row[pl.ds(h * CW + 128 * j, 128)].reshape(1, 128)

        pltpu.make_async_copy(ydst.at[t], ydst.at[t], yrecv.at[t]).wait()
        sums = ysrc[t, :, 0:ROWS]
        for d in range(7):
            sums = sums + ydst[t, d, :, 0:ROWS]
        r2 = two_rows(rm_ref[...] / sums)

        for other in (1, 0):
            h = core + other * (1 - 2 * core)
            part = jnp.dot(r2, k_ref[:, pl.ds(pl.multiple_of(h * CW, CW), CW)], preferred_element_type=F32)
            part = part[0:1] + part[1:2]
            for j in range(TILES):
                xsrc[t, other, j:j + 1, :] = part[:, 128 * j:128 * (j + 1)]
            for to, dx, dz in GROUP:
                if to == other:
                    pltpu.make_async_remote_copy(
                        xsrc.at[t, other], xdst.at[t, GROUP.index((to, dx, dz))], xsend.at[t], xrecv.at[t],
                        device_id=gpeer(to, dx, dz), device_id_type=MESH).start()

        @pl.when(t == ITERS - 1)
        def _():
            r_over = two_rows(1.0 / sums)
            rb_ref[...] = lax.dot_general(r_over, jnp.ones((8, 128), BF16), TN, preferred_element_type=F32)

            def scale_rows(i, carry):
                s = pl.ds(pl.multiple_of(i * 32, 32), 32)
                rb = rb_ref[s, :]
                for q in range(COLS // 128):
                    kr_ref[s, 128 * q:128 * (q + 1)] = k_ref[s, 128 * q:128 * (q + 1)].astype(F32) * rb
                return carry

            lax.fori_loop(0, ROWS // 32, scale_rows, 0)

        pltpu.make_async_copy(xdst.at[t], xdst.at[t], xrecv.at[t]).wait()
        total = xsrc[t, 0]
        for i in range(len(GROUP)):
            total = total + xdst[t, i]
        zsrc[t] = total
        for k, other in ((3, 1), (3, 0), (2, 1), (2, 0), (1, 1), (1, 0), (0, 1)):
            pltpu.make_async_remote_copy(zsrc.at[t], zdst.at[t, other, k], zsend.at[t], zrecv.at[t, other],
                                         device_id=zpeer(other, k), device_id_type=MESH).start()
        sums = jnp.zeros((8, ROWS), F32)
        for other in (0, 1):
            h = core + other * (1 - 2 * core)
            here = zdst.at[t, other, pl.ds(1 - other, 3 + other)]
            pltpu.make_async_copy(here, here, zrecv.at[t, other]).wait()
            total = zdst[t, other, 0] if other else zsrc[t]
            for k in (1, 2, 3):
                total = total + zdst[t, other, k]
            hi, rest = split2(cm_ref[h] / total)
            c2[0] = hi
            c2[1] = rest
            for j in range(TILES):
                lanes = pl.ds(pl.multiple_of(h * CW + 128 * j, 128), 128)
                left[0:1, lanes] = c2[0, j:j + 1, :]
                left[1:2, lanes] = c2[1, j:j + 1, :]
            lanes = pl.ds(pl.multiple_of(h * CW, CW), CW)
            part = lax.dot_general(left[:, lanes].astype(BF16), k_ref[:, lanes], NT, preferred_element_type=F32)
            if other == 0:
                sums = part
            else:
                sums = sums + part

        @pl.when(t < ITERS - 1)
        def _():
            ysrc[t + 1, :, 0:ROWS] = sums[0:1] + sums[1:2]

        return carry

    lax.fori_loop(0, ITERS, iteration, 0)

    def hop(p, s):
        i = tree(p).index(s)
        dest = lax.rem(y - s + 8, 8)
        return pltpu.make_async_remote_copy(
            t_ref.at[dest, pl.ds(p * PR, PR)], rbuf.at[p, i], fsend.at[p, i], frecv.at[p, i],
            device_id=ypeer((parent(s) - s) % 8), device_id_type=MESH)

    def add_arrived(p, s, total):
        for child in tree(p):
            if parent(child) == s:
                i = tree(p).index(child)
                pltpu.make_async_copy(rbuf.at[p, i], rbuf.at[p, i], frecv.at[p, i]).wait()
                total = total + rbuf[p, i]
        return total

    slab_copy.wait()
    for h in (0, 1):
        top = h * ROWS // 2

        def product(i, carry, top=top):
            s = pl.ds(pl.multiple_of(i * KC, KC), KC)
            scale = left[0:1, s] + left[1:2, s]
            plan = (kr_ref[top:top + ROWS // 2, s] * scale).astype(BF16)
            part = jnp.dot(plan, slab_v[s, :], preferred_element_type=F32)

            @pl.when(i == 0)
            def _():
                acc_ref[...] = part

            @pl.when(i > 0)
            def _():
                acc_ref[...] += part

            return carry

        lax.fori_loop(0, COLS // KC, product, 0)

        def pack(i, carry, h=h):
            rows = pl.ds(pl.multiple_of(i * 16, 16), 16)
            below = pl.ds(pl.multiple_of(i * 16 + ROWS // 4, 16), 16)
            to = pl.ds(pl.multiple_of(h * (ROWS // 4) + i * 16, 16), 16)
            for p in range(NY // 2):
                lanes = slice(128 * p, 128 * (p + 1))
                upper, lower = acc_ref[rows, lanes], acc_ref[below, lanes]
                t_ref[2 * p, to, :] = jnp.concatenate([upper[:, :OWN], lower[:, :OWN]], axis=1)
                t_ref[2 * p + 1, to, :] = jnp.concatenate([upper[:, OWN:], lower[:, OWN:]], axis=1)
            return carry

        lax.fori_loop(0, ROWS // 64, pack, 0)
        for m in (4, 3):
            for p in (2 * h, 2 * h + 1):
                for s in (-m, m):
                    if s in tree(p):
                        hop(p, s).start()

    for m in (2, 1):
        for p in range(4):
            for s in (-m, m):
                rows = slice(p * PR, (p + 1) * PR)
                dest = lax.rem(y - s + 8, 8)
                t_ref[dest, rows, :] = add_arrived(p, s, t_ref[dest, rows, :])
                hop(p, s).start()
    for p in range(4):
        total = add_arrived(p, 0, t_ref[y, p * PR:(p + 1) * PR, :]).astype(BF16)
        top = (p // 2) * (ROWS // 2) + (p % 2) * PR
        out_ref[top:top + PR, :] = total[:, :OWN]
        out_ref[top + ROWS // 4:top + ROWS // 4 + PR, :] = total[:, OWN:]

    for t in range(ITERS):
        pltpu.make_async_copy(ydst.at[t], ydst.at[t], ysend.at[t]).wait()
        pltpu.make_async_copy(xdst.at[t], xdst.at[t], xsend.at[t]).wait()
        sent = zdst.at[t, 0, pl.ds(1, 3)]
        pltpu.make_async_copy(sent, sent, zsend.at[t]).wait()
        pltpu.make_async_copy(zdst.at[t, 1], zdst.at[t, 1], zsend.at[t]).wait()
    for p in range(4):
        for s in tree(p):
            hop(p, s).wait_send()


def on_device(cost, row_mass, col_mass, slab):
    hbm = pl.BlockSpec(memory_space=pltpu.HBM)
    dma = pltpu.SemaphoreType.DMA
    return pl.pallas_call(
        kernel,
        out_shape=jax.ShapeDtypeStruct((ROWS, OWN), BF16),
        in_specs=[hbm, hbm, hbm, hbm],
        out_specs=pl.BlockSpec(memory_space=pltpu.VMEM),
        scratch_shapes=[
            pltpu.VMEM((ROWS, COLS), BF16),
            pltpu.VMEM((ROWS, COLS), F32),
            pltpu.VMEM((COLS, SLAB), BF16),
            pltpu.VMEM((ROWS // 2, SLAB), F32),
            pltpu.VMEM((NY, ROWS // 2, 128), F32),
            pltpu.VMEM((4, 7, PR, 128), F32),
            pltpu.VMEM((ROWS, 128), F32),
            pltpu.VMEM((ROWS, 128), F32),
            pltpu.VMEM((2, TR, 128), F32),
            pltpu.VMEM((8, COLS), F32),
            pltpu.VMEM((1, ROWS), F32),
            pltpu.VMEM((COLS,), F32),
            pltpu.VMEM((2, TR, 128), F32),
            pltpu.VMEM((ITERS, 1, 512), F32),
            pltpu.VMEM((ITERS, 7, 1, 512), F32),
            pltpu.VMEM((ITERS, 2, TR, 128), F32),
            pltpu.VMEM((ITERS, len(GROUP), TR, 128), F32),
            pltpu.VMEM((ITERS, TR, 128), F32),
            pltpu.VMEM((ITERS, 2, 4, TR, 128), F32),
            dma((LOADS,)), dma, dma((2,)),
            dma((ITERS,)), dma((ITERS,)),
            dma((ITERS,)), dma((ITERS,)),
            dma((ITERS,)), dma((ITERS, 2)),
            dma((4, 7)), dma((4, 7)),
        ],
        compiler_params=pltpu.CompilerParams(
            collective_id=0, has_side_effects=True, vmem_limit_bytes=60 * 2**20),
    )(cost, row_mass.reshape(1, ROWS), col_mass, slab)


def solution(mesh):
    return jax.shard_map(
        on_device,
        mesh=mesh,
        in_specs=(P("rows", "cols"), P("rows"), P("cols"), P("cols", None)),
        out_specs=P("rows", "cols"),
        check_vma=False,
    )
```

time: 98.6 us -> 90.9 us (0.922)
  Pallas kernels: 94.2 us -> 88.9 us
  local copies, waits for them, and re-layouts: 4.04 us -> 1.62 us
    pallas_call x1, Pallas kernels: 94.2 us -> 88.9 us  [on_device(): pl.pallas_call(kernel, out_shape=jax.ShapeDtypeStruct((ROWS, OWN), BF16),...]
    unnamed x4 -> x0, local copies, waits for them, and re-layouts: 2.59 us -> none
where the time goes in v2:
time: 90.9 us; the launch traced here: 90.5 us
  Pallas kernels  88.9 us (98%)
  local copies, waits for them, and re-layouts  1.62 us (2%)
    pallas_call x1, Pallas kernels, on_device(): pl.pallas_call(kernel, out_shape=jax.ShapeDtypeStruct((ROWS, OWN), BF16),...  88.9 us

profile of v2, /device:TPU:6, one launch (start us, length us, event | category | flops | bytes accessed | tf_op | source)
XLA Modules:
  0.0 90.5 jit_solution(12896672076461052626)
XLA Ops:
  0.0 88.9 %shard_map.46 = bf16[448,64]{1,0:T(8,128)(2,1)} custom-call(bf16[448,3584]{1,0:T(8,128)(2,1)} %cost_ref.1, f32[1,448]{1,0:T(1,128)} %bitcast.1, f32[3584]{0:T(1024)} %cm_hbm.1, bf16[3584,512]{1,0:T(8,128)(2,1)} %slab_ref.1), custom_call_target="tpu_custom_call" | custom-call | tf_op jit(solution)/shard_map/pallas_call | solution.py:297
  88.9 1.6 %copy.5 = bf16[448,64]{0,1:T(8,128)(2,1)} copy(bf16[448,64]{1,0:T(8,128)(2,1)} %shard_map.46) | data formatting | bytes 114688 | tf_op jit(solution)/shard_map/pallas_call | solution.py:297

commit v3 on v2

--- a/solution.py
+++ b/solution.py
@@ -12,7 +12,6 @@
 MESH = pl.DeviceIdType.MESH
 F32, BF16 = jnp.float32, jnp.bfloat16
 NT = (((1,), (1,)), ((), ()))
-TN = (((0,), (0,)), ((), ()))
 
 ROWS, COLS, SLAB = 448, 3584, 512
 NY = 8
@@ -22,8 +21,9 @@
 TR = 16
 LOADS = 7
 LR = ROWS // LOADS
-KC = 896
-PR = ROWS // 8
+KC = 1792
+PR = OWN // 4
+BLOCKS = (4, 3, 5, 2, 6, 1, 7, 0)
 ORDER = (4, 3, 5, 2, 6, 1, 7)
 GROUP = tuple((other, dx, dz) for other in (0, 1) for dx, dz in
               ((2, 1), (2, 0), (1, 1), (3, 1), (1, 0), (3, 0), (0, 1), (0, 0)) if (other, dx, dz) != (0, 0, 0))
@@ -46,7 +46,7 @@
 
 
 def kernel(cost_ref, rm_hbm, cm_hbm, slab_ref, out_ref,
-           k_ref, kr_ref, slab_v, acc_ref, t_ref, rbuf, racc, rb_ref, c2, left, rm_ref, cm_row, cm_ref,
+           k_ref, kt_ref, slab_v, slab_t, t_ref, rbuf, racc, over_ref, c2, left, rm_ref, cm_row, cm_ref,
            ysrc, ydst, xsrc, xdst, zsrc, zdst,
            cost_sem, slab_sem, mass_sem, ysend, yrecv, xsend, xrecv, zsend, zrecv, fsend, frecv):
     r = lax.axis_index("rows")
@@ -141,6 +141,13 @@
             for h in range(2):
                 for j in range(TILES):
                     cm_ref[h, j:j + 1, :] = cm_row[pl.ds(h * CW + 128 * j, 128)].reshape(1, 128)
+
+            def turn(i, carry):
+                s = pl.ds(pl.multiple_of(i * 512, 512), 512)
+                kt_ref[s, :] = k_ref[:, s].T
+                return carry
+
+            lax.fori_loop(0, COLS // 512, turn, 0)
 
         pltpu.make_async_copy(ydst.at[t], ydst.at[t], yrecv.at[t]).wait()
         sums = ysrc[t, :, 0:ROWS]
@@ -162,17 +169,7 @@
 
         @pl.when(t == ITERS - 1)
         def _():
-            r_over = two_rows(1.0 / sums)
-            rb_ref[...] = lax.dot_general(r_over, jnp.ones((8, 128), BF16), TN, preferred_element_type=F32)
-
-            def scale_rows(i, carry):
-                s = pl.ds(pl.multiple_of(i * 32, 32), 32)
-                rb = rb_ref[s, :]
-                for q in range(COLS // 128):
-                    kr_ref[s, 128 * q:128 * (q + 1)] = k_ref[s, 128 * q:128 * (q + 1)].astype(F32) * rb
-                return carry
-
-            lax.fori_loop(0, ROWS // 32, scale_rows, 0)
+            over_ref[...] = 1.0 / sums
 
         pltpu.make_async_copy(xdst.at[t], xdst.at[t], xrecv.at[t]).wait()
         total = xsrc[t, 0]
@@ -182,6 +179,24 @@
         for k, other in ((3, 1), (3, 0), (2, 1), (2, 0), (1, 1), (1, 0), (0, 1)):
             pltpu.make_async_remote_copy(zsrc.at[t], zdst.at[t, other, k], zsend.at[t], zrecv.at[t, other],
                                          device_id=zpeer(other, k), device_id_type=MESH).start()
+
+        @pl.when(t == 0)
+        def _():
+            lane = lax.broadcasted_iota(jnp.int32, (SLAB, 1), 0)
+            source = jnp.zeros((SLAB, 1), jnp.int32)
+            for i, e in enumerate(BLOCKS):
+                first_lane = lax.rem(y + e, 8) * OWN
+                source = jnp.where(lane // OWN == i, first_lane + lane - i * OWN, source)
+            moved = (lax.broadcasted_iota(jnp.int32, (SLAB, SLAB), 1) == source).astype(F32).astype(BF16)
+            slab_copy.wait()
+
+            def reorder(i, carry):
+                s = pl.ds(pl.multiple_of(i * 512, 512), 512)
+                slab_t[:, s] = lax.dot_general(moved, slab_v[s, :], NT, preferred_element_type=F32).astype(BF16)
+                return carry
+
+            lax.fori_loop(0, COLS // 512, reorder, 0)
+
         sums = jnp.zeros((8, ROWS), F32)
         for other in (0, 1):
             h = core + other * (1 - 2 * core)
@@ -198,7 +213,7 @@
                 left[0:1, lanes] = c2[0, j:j + 1, :]
                 left[1:2, lanes] = c2[1, j:j + 1, :]
             lanes = pl.ds(pl.multiple_of(h * CW, CW), CW)
-            part = lax.dot_general(left[:, lanes].astype(BF16), k_ref[:, lanes], NT, preferred_element_type=F32)
+            part = jnp.dot(left[:, lanes].astype(BF16), kt_ref[lanes, :], preferred_element_type=F32)
             if other == 0:
                 sums = part
             else:
@@ -212,11 +227,13 @@
 
     lax.fori_loop(0, ITERS, iteration, 0)
 
+    def piece(e, p):
+        return pl.ds(BLOCKS.index(e % 8) * OWN + p * PR, PR)
+
     def hop(p, s):
         i = tree(p).index(s)
-        dest = lax.rem(y - s + 8, 8)
         return pltpu.make_async_remote_copy(
-            t_ref.at[dest, pl.ds(p * PR, PR)], rbuf.at[p, i], fsend.at[p, i], frecv.at[p, i],
+            t_ref.at[piece(-s, p)], rbuf.at[p, i], fsend.at[p, i], frecv.at[p, i],
             device_id=ypeer((parent(s) - s) % 8), device_id_type=MESH)
 
     def add_arrived(p, s, total):
@@ -227,58 +244,41 @@
                 total = total + rbuf[p, i]
         return total
 
-    slab_copy.wait()
-    for h in (0, 1):
-        top = h * ROWS // 2
-
-        def product(i, carry, top=top):
+    for quarter in range(4):
+        block_rows = slice(quarter * 128, quarter * 128 + 128)
+
+        def product(i, carry, block_rows=block_rows):
             s = pl.ds(pl.multiple_of(i * KC, KC), KC)
             scale = left[0:1, s] + left[1:2, s]
-            plan = (kr_ref[top:top + ROWS // 2, s] * scale).astype(BF16)
-            part = jnp.dot(plan, slab_v[s, :], preferred_element_type=F32)
+            scaled = (slab_t[block_rows, s].astype(F32) * scale).astype(BF16)
+            part = jnp.dot(scaled, kt_ref[s, :], preferred_element_type=F32)
 
             @pl.when(i == 0)
             def _():
-                acc_ref[...] = part
+                t_ref[block_rows, :] = part
 
             @pl.when(i > 0)
             def _():
-                acc_ref[...] += part
+                t_ref[block_rows, :] += part
 
             return carry
 
         lax.fori_loop(0, COLS // KC, product, 0)
-
-        def pack(i, carry, h=h):
-            rows = pl.ds(pl.multiple_of(i * 16, 16), 16)
-            below = pl.ds(pl.multiple_of(i * 16 + ROWS // 4, 16), 16)
-            to = pl.ds(pl.multiple_of(h * (ROWS // 4) + i * 16, 16), 16)
-            for p in range(NY // 2):
-                lanes = slice(128 * p, 128 * (p + 1))
-                upper, lower = acc_ref[rows, lanes], acc_ref[below, lanes]
-                t_ref[2 * p, to, :] = jnp.concatenate([upper[:, :OWN], lower[:, :OWN]], axis=1)
-                t_ref[2 * p + 1, to, :] = jnp.concatenate([upper[:, OWN:], lower[:, OWN:]], axis=1)
-            return carry
-
-        lax.fori_loop(0, ROWS // 64, pack, 0)
-        for m in (4, 3):
-            for p in (2 * h, 2 * h + 1):
-                for s in (-m, m):
+        for m in ((4, -3), (3,), (), ())[quarter]:
+            for p in range(4):
+                for s in ((-4, 4) if m == 4 else (m,)):
                     if s in tree(p):
                         hop(p, s).start()
 
     for m in (2, 1):
         for p in range(4):
             for s in (-m, m):
-                rows = slice(p * PR, (p + 1) * PR)
-                dest = lax.rem(y - s + 8, 8)
-                t_ref[dest, rows, :] = add_arrived(p, s, t_ref[dest, rows, :])
+                rows = piece(-s, p)
+                t_ref[rows, :] = add_arrived(p, s, t_ref[rows, :])
                 hop(p, s).start()
     for p in range(4):
-        total = add_arrived(p, 0, t_ref[y, p * PR:(p + 1) * PR, :]).astype(BF16)
-        top = (p // 2) * (ROWS // 2) + (p % 2) * PR
-        out_ref[top:top + PR, :] = total[:, :OWN]
-        out_ref[top + ROWS // 4:top + ROWS // 4 + PR, :] = total[:, OWN:]
+        total = add_arrived(p, 0, t_ref[piece(0, p), :])
+        out_ref[p * PR:(p + 1) * PR, :] = (total * over_ref[...]).astype(BF16)
 
     for t in range(ITERS):
         pltpu.make_async_copy(ydst.at[t], ydst.at[t], ysend.at[t]).wait()
@@ -296,18 +296,18 @@
     dma = pltpu.SemaphoreType.DMA
     return pl.pallas_call(
         kernel,
-        out_shape=jax.ShapeDtypeStruct((ROWS, OWN), BF16),
+        out_shape=jax.ShapeDtypeStruct((OWN, ROWS), BF16),
         in_specs=[hbm, hbm, hbm, hbm],
         out_specs=pl.BlockSpec(memory_space=pltpu.VMEM),
         scratch_shapes=[
             pltpu.VMEM((ROWS, COLS), BF16),
-            pltpu.VMEM((ROWS, COLS), F32),
+            pltpu.VMEM((COLS, ROWS), BF16),
             pltpu.VMEM((COLS, SLAB), BF16),
-            pltpu.VMEM((ROWS // 2, SLAB), F32),
-            pltpu.VMEM((NY, ROWS // 2, 128), F32),
-            pltpu.VMEM((4, 7, PR, 128), F32),
+            pltpu.VMEM((SLAB, COLS), BF16),
+            pltpu.VMEM((SLAB, ROWS), F32),
+            pltpu.VMEM((4, 7, PR, ROWS), F32),
             pltpu.VMEM((ROWS, 128), F32),
-            pltpu.VMEM((ROWS, 128), F32),
+            pltpu.VMEM((1, ROWS), F32),
             pltpu.VMEM((2, TR, 128), F32),
             pltpu.VMEM((8, COLS), F32),
             pltpu.VMEM((1, ROWS), F32),
@@ -327,7 +327,7 @@
         ],
         compiler_params=pltpu.CompilerParams(
             collective_id=0, has_side_effects=True, vmem_limit_bytes=60 * 2**20),
-    )(cost, row_mass.reshape(1, ROWS), col_mass, slab)
+    )(cost, row_mass.reshape(1, ROWS), col_mass, slab).T
 
 
 def solution(mesh):

time: 90.9 us -> 88.7 us (0.976)
  Pallas kernels: 88.9 us -> 86.9 us
    pallas_call x1, Pallas kernels: 88.9 us -> 86.9 us  [on_device(): pl.pallas_call(kernel, out_shape=jax.ShapeDtypeStruct((OWN, ROWS), BF16),...]
    pallas_call x1 -> x0, local copies, waits for them, and re-layouts: 1.62 us -> none  [on_device(): pl.pallas_call(kernel, out_shape=jax.ShapeDtypeStruct((ROWS, OWN), BF16),...]
    unnamed x0 -> x1, local copies, waits for them, and re-layouts: none -> 1.47 us
where the time goes in v3:
time: 88.7 us; the launch traced here: 88.4 us
  Pallas kernels  86.9 us (98%)
  local copies, waits for them, and re-layouts  1.47 us (2%)
    pallas_call x1, Pallas kernels, on_device(): pl.pallas_call(kernel, out_shape=jax.ShapeDtypeStruct((OWN, ROWS), BF16),...  86.9 us

profile of v3, /device:TPU:6, one launch (start us, length us, event | category | flops | bytes accessed | tf_op | source)
XLA Modules:
  0.0 88.4 jit_solution(1354216462861897373)
XLA Ops:
  0.0 86.9 %shard_map.46 = bf16[64,448]{1,0:T(8,128)(2,1)} custom-call(bf16[448,3584]{1,0:T(8,128)(2,1)} %cost_ref.1, f32[1,448]{1,0:T(1,128)} %bitcast.3, f32[3584]{0:T(1024)} %cm_hbm.1, bf16[3584,512]{1,0:T(8,128)(2,1)} %slab_ref.1), custom_call_target="tpu_custom_call" | custom-call | tf_op jit(solution)/shard_map/pallas_call | solution.py:297
  86.9 1.5 %copy.6 = bf16[448,64]{0,1:T(8,128)(2,1)} copy(bf16[448,64]{0,1:T(8,128)(2,1)} %bitcast.2) | data formatting | bytes 114688

commit v4 on v3

--- a/solution.py
+++ b/solution.py
@@ -27,6 +27,7 @@
 ORDER = (4, 3, 5, 2, 6, 1, 7)
 GROUP = tuple((other, dx, dz) for other in (0, 1) for dx, dz in
               ((2, 1), (2, 0), (1, 1), (3, 1), (1, 0), (3, 0), (0, 1), (0, 0)) if (other, dx, dz) != (0, 0, 0))
+FARTHEST = sorted(range(len(GROUP)), key=lambda i: -2 * (2 - abs(GROUP[i][1] - 2)) - GROUP[i][2])
 
 
 def parent(s):
@@ -155,24 +156,23 @@
             sums = sums + ydst[t, d, :, 0:ROWS]
         r2 = two_rows(rm_ref[...] / sums)
 
-        for other in (1, 0):
+        part = jnp.dot(r2, k_ref[...], preferred_element_type=F32)
+        part = part[0:1] + part[1:2]
+        for h in (0, 1):
+            for j in range(TILES):
+                xsrc[t, h, j:j + 1, :] = part[:, h * CW + 128 * j:h * CW + 128 * (j + 1)]
+        for i in FARTHEST:
+            other, dx, dz = GROUP[i]
             h = core + other * (1 - 2 * core)
-            part = jnp.dot(r2, k_ref[:, pl.ds(pl.multiple_of(h * CW, CW), CW)], preferred_element_type=F32)
-            part = part[0:1] + part[1:2]
-            for j in range(TILES):
-                xsrc[t, other, j:j + 1, :] = part[:, 128 * j:128 * (j + 1)]
-            for to, dx, dz in GROUP:
-                if to == other:
-                    pltpu.make_async_remote_copy(
-                        xsrc.at[t, other], xdst.at[t, GROUP.index((to, dx, dz))], xsend.at[t], xrecv.at[t],
-                        device_id=gpeer(to, dx, dz), device_id_type=MESH).start()
+            pltpu.make_async_remote_copy(xsrc.at[t, h], xdst.at[t, i], xsend.at[t], xrecv.at[t],
+                                         device_id=gpeer(other, dx, dz), device_id_type=MESH).start()
 
         @pl.when(t == ITERS - 1)
         def _():
             over_ref[...] = 1.0 / sums
 
         pltpu.make_async_copy(xdst.at[t], xdst.at[t], xrecv.at[t]).wait()
-        total = xsrc[t, 0]
+        total = xsrc[t, core]
         for i in range(len(GROUP)):
             total = total + xdst[t, i]
         zsrc[t] = total
@@ -296,7 +296,7 @@
     dma = pltpu.SemaphoreType.DMA
     return pl.pallas_call(
         kernel,
-        out_shape=jax.ShapeDtypeStruct((OWN, ROWS), BF16),
+        out_shape=pltpu.VMEM((OWN, ROWS), BF16),
         in_specs=[hbm, hbm, hbm, hbm],
         out_specs=pl.BlockSpec(memory_space=pltpu.VMEM),
         scratch_shapes=[

time: 88.7 us -> 87.1 us (0.982)
  Pallas kernels: 86.9 us -> 85.8 us
    pallas_call x1, Pallas kernels: 86.9 us -> 85.8 us  [on_device(): pl.pallas_call(kernel, out_shape=pltpu.VMEM((OWN, ROWS), BF16), in_specs=...]
where the time goes in v4:
time: 87.1 us; the launch traced here: 86.5 us
  Pallas kernels  85.8 us (99%)
    pallas_call x1, Pallas kernels, on_device(): pl.pallas_call(kernel, out_shape=pltpu.VMEM((OWN, ROWS), BF16), in_specs=...  85.8 us

profile of v4, /device:TPU:6, one launch (start us, length us, event | category | flops | bytes accessed | tf_op | source)
XLA Modules:
  0.0 86.5 jit_solution(4410235459402878021)
XLA Ops:
  0.0 85.8 %shard_map.46 = bf16[64,448]{1,0:T(8,128)(2,1)S(1)} custom-call(bf16[448,3584]{1,0:T(8,128)(2,1)} %cost_ref.1, f32[1,448]{1,0:T(1,128)} %bitcast.3, f32[3584]{0:T(1024)} %cm_hbm.1, bf16[3584,512]{1,0:T(8,128)(2,1)} %slab_ref.1), custom_call_target="tpu_custom_call" | custom-call | tf_op jit(solution)/shard_map/pallas_call | solution.py:297
  85.9 0.6 copy.6

commit v5 on v4

--- a/solution.py
+++ b/solution.py
@@ -197,7 +197,6 @@
 
             lax.fori_loop(0, COLS // 512, reorder, 0)
 
-        sums = jnp.zeros((8, ROWS), F32)
         for other in (0, 1):
             h = core + other * (1 - 2 * core)
             here = zdst.at[t, other, pl.ds(1 - other, 3 + other)]
@@ -212,15 +211,10 @@
                 lanes = pl.ds(pl.multiple_of(h * CW + 128 * j, 128), 128)
                 left[0:1, lanes] = c2[0, j:j + 1, :]
                 left[1:2, lanes] = c2[1, j:j + 1, :]
-            lanes = pl.ds(pl.multiple_of(h * CW, CW), CW)
-            part = jnp.dot(left[:, lanes].astype(BF16), kt_ref[lanes, :], preferred_element_type=F32)
-            if other == 0:
-                sums = part
-            else:
-                sums = sums + part
 
         @pl.when(t < ITERS - 1)
         def _():
+            sums = jnp.dot(left[...].astype(BF16), kt_ref[...], preferred_element_type=F32)
             ysrc[t + 1, :, 0:ROWS] = sums[0:1] + sums[1:2]
 
         return carry

time: 87.1 us -> 86.2 us (0.990)
  Pallas kernels: 85.8 us -> 84.8 us
    pallas_call x1, Pallas kernels: 85.8 us -> 84.8 us  [on_device(): pl.pallas_call(kernel, out_shape=pltpu.VMEM((OWN, ROWS), BF16), in_specs=...]
where the time goes in v5:
time: 86.2 us; the launch traced here: 85.5 us
  Pallas kernels  84.8 us (98%)
    pallas_call x1, Pallas kernels, on_device(): pl.pallas_call(kernel, out_shape=pltpu.VMEM((OWN, ROWS), BF16), in_specs=...  84.8 us

profile of v5, /device:TPU:6, one launch (start us, length us, event | category | flops | bytes accessed | tf_op | source)
XLA Modules:
  0.0 85.5 jit_solution(6744910310333687058)
XLA Ops:
  0.0 84.8 %shard_map.46 = bf16[64,448]{1,0:T(8,128)(2,1)S(1)} custom-call(bf16[448,3584]{1,0:T(8,128)(2,1)} %cost_ref.1, f32[1,448]{1,0:T(1,128)} %bitcast.3, f32[3584]{0:T(1024)} %cm_hbm.1, bf16[3584,512]{1,0:T(8,128)(2,1)} %slab_ref.1), custom_call_target="tpu_custom_call" | custom-call | tf_op jit(solution)/shard_map/pallas_call | solution.py:291
  84.8 0.6 copy.6
